TPU v7x, 32 devices: a whole 2x2x4 slice. The times are simulated.
32 devices in a mesh: ctx: 4 (over x, core), row: 4 (over z), col: 2 (over y).
Axes of the slice: x: 2, y: 2, z: 4, core: 2. Of those that a mesh axis runs over, the one named last changes fastest.
Arguments:
- inputs: bfloat16 [1024, 4096], P('ctx', 'col'), may hold values from -12 to 12
- qkv_weight: bfloat16 [4096, 6144], P('col', 'row'), may hold values from -0.140625 to 0.140625
- out_cotangent: bfloat16 [1024, 2048], P('ctx', ('row', 'col')), may hold values from -6 to 6
Outputs:
- attended: bfloat16 [1024, 2048], P('ctx', ('row', 'col'))
- input_grad: bfloat16 [1024, 4096], P('ctx', 'col')
All inputs are finite; a program needn't handle non-finite values.
Results may differ from a plain program's by a relative error of at most 0.0173.
The roundings to bfloat16 on the way count: a program that leaves them out, or rounds other values in their place, can miss the bound.
Values may be sent and summed in bfloat16 or wider, within the bound.
A program may use at most 128 MiB of HBM per device.

v0:
```python
import math

import jax
import jax.numpy as jnp
from jax import lax
from jax.sharding import PartitionSpec as P

DH = 128


def softmax_rows(scores):
    row_top = jnp.max(scores, axis=2)
    expo_vals = jnp.exp(scores - row_top[:, :, None])
    row_total = jnp.sum(expo_vals, axis=2)
    return (row_top, row_total, expo_vals / row_total[:, :, None])


def shards(inputs, qkv_weight, out_cotangent):
    tok_rows = inputs.shape[0]
    scaling = 1.0 / math.sqrt(DH)
    per_device = qkv_weight.shape[1] // lax.axis_size("col")
    local_heads = per_device // (3 * DH)
    panel_cols = qkv_weight
    packed = lax.psum_scatter(
        lax.dot_general(
            panel_cols, inputs, (((0,), (1,)), ((), ())), preferred_element_type=jnp.float32
        ),
        "col",
        scatter_dimension=0,
        tiled=True,
    ).astype(jnp.bfloat16)
    packed = packed.reshape(local_heads, 3, DH, tok_rows)
    queries = packed[:, 0]
    key_own = packed[:, 1]
    value_own = packed[:, 2]
    gathered = lax.all_gather(jnp.stack([key_own, value_own]), "ctx", axis=3, tiled=True)
    keys_all = gathered[0]
    values_all = gathered[1]
    scores = (
        jnp.einsum("hdq,hdk->hqk", queries, keys_all, preferred_element_type=jnp.float32) * scaling
    )
    row_top, row_total, softmax = softmax_rows(scores)
    softmax_low = softmax.astype(jnp.bfloat16)
    attended3 = jnp.einsum(
        "hqk,hdk->qhd", softmax_low, values_all, preferred_element_type=jnp.float32
    ).astype(jnp.bfloat16)
    attended = attended3.reshape(tok_rows, local_heads * DH)
    grad_out = out_cotangent.reshape(tok_rows, local_heads, DH)
    row_delta = jnp.sum(grad_out.astype(jnp.float32) * attended3.astype(jnp.float32), axis=2).T
    grad_soft = jnp.einsum("qhd,hdk->hqk", grad_out, values_all, preferred_element_type=jnp.float32)
    grad_score = (softmax * (grad_soft - row_delta[:, :, None])).astype(jnp.bfloat16)
    grad_query = (
        jnp.einsum("hqk,hdk->hdq", grad_score, keys_all, preferred_element_type=jnp.float32)
        * scaling
    ).astype(jnp.bfloat16)
    grad_out_t = jnp.transpose(grad_out, (1, 2, 0))
    stat_top, stat_total, stat_delta = (
        lax.all_gather(row_top, "ctx", axis=1, tiled=True),
        lax.all_gather(row_total, "ctx", axis=1, tiled=True),
        lax.all_gather(row_delta, "ctx", axis=1, tiled=True),
    )
    query_part = lax.all_gather(queries, "ctx", axis=2, tiled=True)
    grad_part = lax.all_gather(grad_out_t, "ctx", axis=2, tiled=True)
    part_scores = (
        jnp.einsum("hdq,hdk->hqk", query_part, key_own, preferred_element_type=jnp.float32)
        * scaling
    )
    part_prob = jnp.exp(part_scores - stat_top[:, :, None]) / stat_total[:, :, None]
    part_grad = jnp.einsum("hdq,hdk->hqk", grad_part, value_own, preferred_element_type=jnp.float32)
    part_score = (part_prob * (part_grad - stat_delta[:, :, None])).astype(jnp.bfloat16)
    new_key = (
        jnp.einsum("hqk,hdq->hdk", part_score, query_part, preferred_element_type=jnp.float32)
        * scaling
    )
    new_value = jnp.einsum(
        "hqk,hdq->hdk",
        part_prob.astype(jnp.bfloat16),
        grad_part,
        preferred_element_type=jnp.float32,
    )
    grad_key = new_key
    grad_value = new_value
    grad_key = grad_key.astype(jnp.bfloat16)
    grad_value = grad_value.astype(jnp.bfloat16)
    grad_packed = jnp.stack([grad_query, grad_key, grad_value], axis=1).reshape(
        local_heads * 3 * DH, tok_rows
    )
    panel_cols = qkv_weight
    local_sum = lax.dot_general(
        lax.all_gather(grad_packed, "col", axis=0, tiled=True),
        panel_cols,
        (((0,), (1,)), ((), ())),
        preferred_element_type=jnp.float32,
    )
    input_grad = lax.psum(local_sum, "row").astype(jnp.bfloat16)
    return (attended, input_grad)


def solution(mesh):
    return jax.shard_map(
        shards,
        mesh=mesh,
        in_specs=(P("ctx", "col"), P("col", "row"), P("ctx", ("row", "col"))),
        out_specs=(P("ctx", ("row", "col")), P("ctx", "col")),
        check_vma=False,
    )
```

profile of v0, /device:TPU:0, one launch (start us, length us, event | category | flops | bytes accessed | tf_op | source)
XLA Modules:
  0.0 195.3 jit_solution(13312935264299797373)
XLA Ops:
  7.2 1.2 copy-done
  8.4 5.8 %fusion.33 = f32[1536,256]{1,0:T(8,128)} fusion(bf16[2048,1536]{1,0:T(8,128)(2,1)} %param.4, bf16[256,2048]{1,0:T(8,128)(2,1)S(1)} %copy-done), kind=kOutput, calls=%fused_computation.43 | convolution fusion | flops 1610612736 | bytes 8912896 | tf_op jit(solution)/shard_map/dot_general | solution.py:25
  14.3 28.9 %reduce-scatter.2.cloned.1.call-done = f32[768,256]{1,0:T(8,128)} async-done(((f32[1536,256]{1,0:T(8,128)}), f32[768,256]{1,0:T(8,128)}) %reduce-scatter.2.cloned.1.call-update) | async-done | bytes 786448 | tf_op jit(solution)/shard_map/reduce_scatter | solution.py:24
  43.1 1.2 convert_element_type.42
  44.4 0.7 pad_maximum_fusion.1
  45.2 7.6 %all_gather.25 = bf16[2,128,1024]{2,1,0:T(8,128)(2,1)} all-gather(bf16[2,128,256]{2,1,0:T(8,128)(2,1)S(1)} %bitcast.96), channel_id=1, replica_groups=mesh['ctx'=4,'row'=4,'col'=2] {'ctx'}, dimensions={2}, use_global_device_ids=true | all-gather | bytes 655360 | tf_op jit(solution)/shard_map/all_gather | solution.py:63
  53.0 10.9 %all-gather = bf16[2,1,128,1024]{2,3,0,1:T(8,128)(2,1)} all-gather(bf16[2,1,128,256]{2,3,0,1:T(8,128)(2,1)S(1)} %copy.21), channel_id=2, replica_groups=mesh['ctx'=4,'row'=4,'col'=2] {'ctx'}, dimensions={3}, use_global_device_ids=true | all-gather | bytes 655360 | tf_op jit(solution)/shard_map/all_gather | solution.py:62
  63.9 1.2 all-gather.3.cloned.1.call-done
  65.0 1.7 multiply_reduce_fusion
  66.7 5.2 %all_gather.23 = f32[2,1024]{1,0:T(2,128)S(1)} all-gather(f32[2,256]{1,0:T(2,128)S(1)} %get-tuple-element.9), channel_id=1, replica_groups=mesh['ctx'=4,'row'=4,'col'=2] {'ctx'}, dimensions={1}, use_global_device_ids=true | all-gather | bytes 10240 | tf_op jit(solution)/shard_map/all_gather | solution.py:58
  71.9 0.5 fusion.3
  72.4 5.2 %all_gather.24 = f32[2,1024]{1,0:T(2,128)S(1)} all-gather(f32[2,256]{1,0:T(2,128)S(1)} %fusion.3), channel_id=1, replica_groups=mesh['ctx'=4,'row'=4,'col'=2] {'ctx'}, dimensions={1}, use_global_device_ids=true | all-gather | bytes 10240 | tf_op jit(solution)/shard_map/all_gather | solution.py:59
  77.6 1.4 multiply_reduce_fusion.1
  78.9 0.6 copy-done.11
  79.5 5.1 %all_gather.26 = f32[2,1024]{1,0:T(2,128)S(1)} all-gather(f32[2,256]{1,0:T(2,128)S(1)} %bitcast.99), channel_id=1, replica_groups=mesh['ctx'=4,'row'=4,'col'=2] {'ctx'}, dimensions={1}, use_global_device_ids=true | all-gather | bytes 10240 | tf_op jit(solution)/shard_map/all_gather | solution.py:60
  84.7 0.8 exponential_divide_fusion
  85.5 1.3 copy-done.1
  86.8 1.0 fusion.10
  87.8 3.4 %fusion.11 = bf16[2,1,128,256]{3,2,0,1:T(8,128)(2,1)} fusion(f32[2,1024,256]{2,1,0:T(8,128)} %copy-done.1, bf16[2,128,1024]{2,1,0:T(8,128)(2,1)} %all_gather.25, f32[2,1024]{1,0:T(2,128)S(1)} %all_gather.26, bf16[2,1,128,1024]{2,3,0,1:T(8,128)(2,1)} %all-gather, bf16[2,3,128,256]{3,2,1,0:T(8,128)(2,1)S(1)} %bitcast.94), kind=kOutput, calls=%fused_computation.18 | convolution fusion | flops 270139392 | bytes 3416064 | tf_op jit(solution)/shard_map/hqk,hdq->hdk/dot_general | solution.py:72
  91.3 2.3 %fusion.12 = bf16[2,1,128,256]{3,2,0,1:T(8,128)(2,1)S(1)} fusion(bf16[256,2,128]{0,2,1:T(8,128)(2,1)} %bitcast.97, f32[2,256]{1,0:T(2,128)} %bitcast.100, f32[2,256,1024]{2,1,0:T(8,128)S(1)} %get-tuple-element.10, f32[2,256]{1,0:T(2,128)S(1)} %fusion.3, f32[2,256]{1,0:T(2,128)S(1)} %get-tuple-element.9, ...), kind=kOutput, calls=%fused_computation.19 | convolution fusion | flops 271712256 | bytes 3414016 | tf_op jit(solution)/shard_map/hqk,hdk->hdq/dot_general | solution.py:53
  93.7 12.0 %all_gather.27 = bf16[1536,256]{1,0:T(8,128)(2,1)S(1)} all-gather(bf16[768,256]{1,0:T(8,128)(2,1)S(1)} %bitcast.95), channel_id=1, replica_groups=mesh['ctx'=4,'row'=4,'col'=2] {'col'}, dimensions={0}, use_global_device_ids=true | all-gather | bytes 1179648 | tf_op jit(solution)/shard_map/all_gather | solution.py:90
  105.7 4.6 %fusion.34 = f32[256,2048]{1,0:T(8,128)S(1)} fusion(bf16[1536,256]{1,0:T(8,128)(2,1)S(1)} %all_gather.27, bf16[2048,1536]{1,0:T(8,128)(2,1)} %param.4), kind=kOutput, calls=%fused_computation.44 | convolution fusion | flops 1610612736 | bytes 9175040 | tf_op jit(solution)/shard_map/dot_general | solution.py:89
  110.4 77.3 %all-reduce.1 = bf16[256,2048]{1,0:T(8,128)(2,1)} all-reduce(f32[256,2048]{1,0:T(8,128)S(1)} %fusion.34), channel_id=1, replica_groups=mesh['ctx'=4,'row'=4,'col'=2] {'row'}, use_global_device_ids=true, to_apply=%region_4.0 | all-reduce | flops 524288 | bytes 3145728 | tf_op jit(solution)/shard_map/psum | solution.py:95
  187.7 0.8 copy.17
  (30 shorter events, 0.5 us)
Async XLA Ops:
  7.2 1.2 copy-start
  7.2 36.0 %reduce-scatter.2.cloned.1.call-start = ((), (), s32[]{:S(2)}) async-start(), calls=%async_computation.1 | async-start | bytes 2359296 | tf_op jit(solution)/shard_map/reduce_scatter | solution.py:24
  14.2 30.9 %copy-start.9 = (bf16[256,256]{1,0:T(8,128)(2,1)S(1)}, bf16[256,256]{1,0:T(8,128)(2,1)}, u32[]{:S(2)}) copy-start(bf16[256,256]{1,0:T(8,128)(2,1)} %param.5) | copy-start | bytes 393220
  14.2 50.8 %all-gather.3.cloned.1.call-start = ((), (), s32[]{:S(2)}) async-start(), calls=%async_computation.2 | async-start | bytes 1310720 | tf_op jit(solution)/shard_map/all_gather | solution.py:36
  45.2 18.6 %copy-start.4 = (bf16[256,256]{0,1:T(8,128)(2,1)}, bf16[256,256]{0,1:T(8,128)(2,1)S(1)}, u32[]{:S(2)}) copy-start(bf16[256,256]{0,1:T(8,128)(2,1)S(1)} %copy.14) | copy-start | bytes 393220
  65.0 12.5 %copy-start.5 = (bf16[256,256]{0,1:T(8,128)(2,1)S(1)}, bf16[256,256]{0,1:T(8,128)(2,1)}, u32[]{:S(2)}) copy-start(bf16[256,256]{0,1:T(8,128)(2,1)} %copy-done.4) | copy-start | bytes 393220
  65.0 12.5 %copy-start.8 = (bf16[2,2,128,1024]{3,2,1,0:T(8,128)(2,1)S(1)}, bf16[2,2,128,1024]{3,2,1,0:T(8,128)(2,1)}, u32[]{:S(2)}) copy-start(bf16[2,2,128,1024]{3,2,1,0:T(8,128)(2,1)} %all-gather.3.cloned.1.call-done) | copy-start | bytes 3145732
  77.6 7.1 %copy-start.3 = (bf16[2,1,128,1024]{2,3,0,1:T(8,128)(2,1)S(1)}, bf16[2,1,128,1024]{2,3,0,1:T(8,128)(2,1)}, u32[]{:S(2)}) copy-start(bf16[2,1,128,1024]{2,3,0,1:T(8,128)(2,1)} %all-gather) | copy-start | bytes 1572868
  78.9 0.6 copy-start.11
  84.7 2.2 %copy-start.2 = (bf16[2,128,1024]{2,1,0:T(8,128)(2,1)S(1)}, bf16[2,128,1024]{2,1,0:T(8,128)(2,1)}, u32[]{:S(2)}) copy-start(bf16[2,128,1024]{2,1,0:T(8,128)(2,1)} %all_gather.25) | copy-start | bytes 1572868
  85.5 1.4 copy-start.1
  91.2 2.4 %copy-start.6 = (bf16[2,1,128,256]{3,2,0,1:T(8,128)(2,1)S(1)}, bf16[2,1,128,256]{3,2,0,1:T(8,128)(2,1)}, u32[]{:S(2)}) copy-start(bf16[2,1,128,256]{3,2,0,1:T(8,128)(2,1)} %fusion.10) | copy-start | bytes 393220
  91.3 2.4 %copy-start.7 = (bf16[2,1,128,256]{3,2,0,1:T(8,128)(2,1)S(1)}, bf16[2,1,128,256]{3,2,0,1:T(8,128)(2,1)}, u32[]{:S(2)}) copy-start(bf16[2,1,128,256]{3,2,0,1:T(8,128)(2,1)} %fusion.11) | copy-start | bytes 393220
  110.4 77.3 %copy-start.10 = (bf16[2,128,256]{2,1,0:T(8,128)(2,1)S(1)}, bf16[2,128,256]{2,1,0:T(8,128)(2,1)}, u32[]{:S(2)}) copy-start(bf16[2,128,256]{2,1,0:T(8,128)(2,1)} %get-tuple-element.12) | copy-start | bytes 393220
Sparse Core Ops, SparseCore 0:
  14.3 28.7 reduce-scatter.1
  45.3 19.6 all-gather.2
where the time goes:
time: 196 us; the launch traced here: 195 us
  blocking collectives  123 us (63%)
  waiting for transfers between devices  30.1 us (15%)
  matrix products  21 us (11%)
  between operations  14.2 us (7%)
  local copies, waits for them, and re-layouts  4.19 us (2%)
  other arithmetic  2.43 us (1%)
    psum x1, blocking collectives, shards(): input_grad = lax.psum(local_sum, 'row').astype(jnp.bfloat16)  77.3 us
    reduce_scatter x1, waiting for transfers between devices, shards(): lax.psum_scatter(lax.dot_general(panel_cols, inputs, (((0,), (1,)), ((),...  28.9 us
    all_gather x1, blocking collectives, shards(): lax.all_gather(grad_packed, 'col', axis=0, tiled=True)  12 us
    all_gather x1, blocking collectives, shards(): query_part = lax.all_gather(queries, 'ctx', axis=2, tiled=True)  10.9 us
    all_gather x1, blocking collectives, shards(): grad_part = lax.all_gather(grad_out_t, 'ctx', axis=2, tiled=True)  7.6 us
    dot_general x1, matrix products, shards(): lax.dot_general(panel_cols, inputs, (((0,), (1,)), ((), ())), preferred_e...  5.79 us
    all_gather x1, blocking collectives, shards(): lax.all_gather(row_total, 'ctx', axis=1, tiled=True)  5.17 us
    all_gather x1, blocking collectives, shards(): lax.all_gather(row_top, 'ctx', axis=1, tiled=True)  5.16 us
  transfers between devices with their start and end apart: 2, of which 2 were waited for; matrix products, arithmetic and copies ran while one was open for 0% of the time, Pallas kernels for 0%

commit v1 on v0

--- a/solution.py
+++ b/solution.py
@@ -3,6 +3,8 @@
 import jax
 import jax.numpy as jnp
 from jax import lax
+from jax.experimental import pallas as pl
+from jax.experimental.pallas import tpu as pltpu
 from jax.sharding import PartitionSpec as P
 
 DH = 128
@@ -96,9 +98,302 @@
     return (attended, input_grad)
 
 
+MESH = pl.DeviceIdType.MESH
+CHUNKS = 16
+NN = (((1,), (0,)), ((), ()))
+NT = (((1,), (1,)), ((), ()))
+TN = (((0,), (0,)), ((), ()))
+
+
+def dot(a, b, dims):
+    return lax.dot_general(a, b, dims, preferred_element_type=jnp.float32)
+
+
+def block_kernel(
+    x_hbm, w_hbm, cot_hbm, att_ref, grad_ref,
+    x_ref, w_ref, cot_ref, far_kv, far_q, got_kv, got_q, part_near, got_near, cot_all, query, kv, score, gscore,
+    prob_low, ds_low, att_mine, att_send, att_got, dq_send, dkv_send, dkv_got, dkv_own,
+    dkv_out, packed, z_own, z_edge, z_mid, z_tot, ss, rs, zs, zr, ls,
+):
+    tok = x_hbm.shape[0]
+    head = 3 * DH
+    scaling = 1.0 / math.sqrt(DH)
+    ctx, row, col = lax.axis_index("ctx"), lax.axis_index("row"), lax.axis_index("col")
+    core = lax.rem(ctx, 2)
+    far_x = lax.rem(ctx + 2, 4)
+    near = ctx + 1 - 2 * core
+    far_col = 1 - col
+    is_mid = jnp.logical_or(row == 1, row == 2)
+    mid_peer = 3 - row
+    side = jnp.where(row == 0, 1, jnp.where(row == 1, 0, jnp.where(row == 2, 3, 2)))
+    at_near = {"ctx": near, "row": row, "col": col}
+    at_far = {"ctx": ctx, "row": row, "col": far_col}
+    at_diag = {"ctx": near, "row": row, "col": far_col}
+    at_x = {"ctx": far_x, "row": row, "col": col}
+    at_side = {"ctx": ctx, "row": side, "col": col}
+    at_mid = {"ctx": ctx, "row": mid_peer, "col": col}
+
+    def rc(src, dst, n, dev):
+        return pltpu.make_async_remote_copy(
+            src_ref=src, dst_ref=dst, send_sem=ss.at[n], recv_sem=rs.at[n],
+            device_id=dev, device_id_type=MESH,
+        )
+
+    def lanes(start, size):
+        return pl.ds(pl.multiple_of(start, 128), size)
+
+    far_w = lanes(far_col * 2 * head, 2 * head)
+    own_w = lanes(col * 2 * head, 2 * head)
+    loads = [
+        pltpu.make_async_copy(x_hbm, x_ref, ls.at[0]),
+        pltpu.make_async_copy(w_hbm.at[:, far_w], w_ref.at[:, far_w], ls.at[1]),
+        pltpu.make_async_copy(w_hbm.at[:, own_w], w_ref.at[:, own_w], ls.at[2]),
+        pltpu.make_async_copy(cot_hbm, cot_ref, ls.at[3]),
+    ]
+    for load in loads:
+        load.start()
+    barrier = pltpu.get_barrier_semaphore()
+    for dev in (at_near, at_far, at_diag, at_x, at_side):
+        pl.semaphore_signal(barrier, inc=1, device_id=dev, device_id_type=MESH)
+
+    @pl.when(is_mid)
+    def _():
+        pl.semaphore_signal(barrier, inc=1, device_id=at_mid, device_id_type=MESH)
+
+    loads[0].wait()
+    loads[1].wait()
+    far = dot(x_ref[...], w_ref[:, far_w], NN)
+    for n in range(2):
+        far_q[n] = far[:, n * head : n * head + DH]
+        far_kv[n] = far[:, n * head + DH : (n + 1) * head]
+
+    @pl.when(is_mid)
+    def _():
+        pl.semaphore_wait(barrier, 6)
+
+    @pl.when(jnp.logical_not(is_mid))
+    def _():
+        pl.semaphore_wait(barrier, 5)
+
+    sent = []
+
+    def go(copy):
+        copy.start()
+        sent.append(copy)
+        return copy
+
+    kv_copies = [go(rc(far_kv.at[core], got_kv.at[0], 0, at_far))]
+    kv_copies.append(go(rc(far_kv.at[1 - core], got_kv.at[1], 1, at_diag)))
+    q_copies = [go(rc(far_q.at[core], got_q.at[0], 15, at_far))]
+    q_copies.append(go(rc(far_q.at[1 - core], got_q.at[1], 16, at_diag)))
+    loads[3].wait()
+    cc = go(rc(cot_ref.at[:, lanes((1 - core) * DH, DH)], cot_all.at[pl.ds(tok, tok)], 3, at_near))
+    loads[2].wait()
+    own = dot(x_ref[...], w_ref[:, own_w], NN)
+    part_near[0] = own[:, :head]
+    part_near[1] = own[:, head:]
+    near_copy = go(rc(part_near.at[1 - core], got_near, 2, at_near))
+    cot_all[pl.ds(0, tok), :] = cot_ref[:, lanes(core * DH, DH)]
+
+    kv_sent = []
+    for t in range(2):
+        kv_copies[t].wait_recv()
+        if t == 0:
+            mine = part_near[core, :, DH:]
+        else:
+            near_copy.wait_recv()
+            mine = got_near[:, DH:]
+        here = pl.ds(t * tok, tok)
+        kv[here, :] = (mine + got_kv[t]).astype(jnp.bfloat16)
+        kv_sent.append(go(rc(kv.at[here], kv.at[pl.ds((2 + t) * tok, tok)], 4 + t, at_x)))
+
+    cc.wait_recv()
+    near_keys = pl.ds(0, 2 * tok)
+    far_keys = pl.ds(2 * tok, 2 * tok)
+    gscore[:, near_keys] = dot(cot_all[...], kv[near_keys, DH:], NT)
+    for t in range(2):
+        q_copies[t].wait_recv()
+        mine = part_near[core, :, :DH] if t == 0 else got_near[:, :DH]
+        query[pl.ds(t * tok, tok), :] = (mine + got_q[t]).astype(jnp.bfloat16)
+    score[:, near_keys] = dot(query[...], kv[near_keys, :DH], NT) * scaling
+    for t in range(2):
+        kv_sent[t].wait_recv()
+    gscore[:, far_keys] = dot(cot_all[...], kv[far_keys, DH:], NT)
+    score[:, far_keys] = dot(query[...], kv[far_keys, :DH], NT) * scaling
+
+    mine_lane = (2 * col + core) * head
+    part = tok // 2
+    for t in (1, 0):
+        for half in range(2):
+            here = pl.ds(t * tok + half * part, part)
+            local = pl.ds(half * part, part)
+            s = score[here, :]
+            e = jnp.exp(s - jnp.max(s, axis=1, keepdims=True))
+            p = e * (1.0 / jnp.sum(e, axis=1, keepdims=True))
+            low = p.astype(jnp.bfloat16)
+            prob_low[here, :] = low
+            att = dot(low, kv[:, DH:], NN).astype(jnp.bfloat16)
+            delta = jnp.sum(
+                cot_all[here, :].astype(jnp.float32) * att.astype(jnp.float32), axis=1, keepdims=True
+            )
+            ds = (p * (gscore[here, :] - delta)).astype(jnp.bfloat16)
+            ds_low[here, :] = ds
+            dq_send[here, :] = (dot(ds, kv[:, :DH], NN) * scaling).astype(jnp.bfloat16)
+            if t == 1:
+                att_send[local, :] = att
+            else:
+                att_mine[local, :] = att
+        here = pl.ds(t * tok, tok)
+        slot = packed.at[:, lanes(mine_lane, DH)]
+        if t == 1:
+            go(rc(dq_send.at[here], slot, 9, at_diag))
+            go(rc(dq_send.at[here], slot, 10, at_near))
+            att_copy = go(rc(att_send, att_got, 8, at_near))
+        else:
+            go(rc(dq_send.at[here], slot, 11, at_far))
+            packed[:, lanes(mine_lane, DH)] = dq_send[here, :]
+
+    dkv_copies = []
+    for t in range(2):
+        keys = pl.ds((2 + t) * tok, tok)
+        here = pl.ds(t * tok, tok)
+        dkv_send[here, :DH] = (dot(ds_low[:, keys], query[...], TN) * scaling).astype(jnp.bfloat16)
+        dkv_send[here, DH:] = dot(prob_low[:, keys], cot_all[...], TN).astype(jnp.bfloat16)
+        dkv_copies.append(go(rc(dkv_send.at[here], dkv_got.at[here], 6 + t, at_x)))
+    dkv_own[:, :DH] = dot(ds_low[:, near_keys], query[...], TN) * scaling
+    dkv_own[:, DH:] = dot(prob_low[:, near_keys], cot_all[...], TN)
+    att_copy.wait_recv()
+    att_ref[:, lanes(core * DH, DH)] = att_mine[...]
+    att_ref[:, lanes((1 - core) * DH, DH)] = att_got[...]
+    slot = packed.at[:, lanes(mine_lane + DH, 2 * DH)]
+    for t in (0, 1):
+        here = pl.ds(t * tok, tok)
+        dkv_copies[t].wait_recv()
+        dkv_out[here, :] = (dkv_own[here, :] + dkv_got[here, :].astype(jnp.float32)).astype(jnp.bfloat16)
+        if t == 1:
+            go(rc(dkv_out.at[here], slot, 12, at_diag))
+            go(rc(dkv_out.at[here], slot, 13, at_near))
+        else:
+            go(rc(dkv_out.at[here], slot, 14, at_far))
+            packed[:, lanes(mine_lane + DH, 2 * DH)] = dkv_out[here, :]
+
+    near_lane = (2 * col + 1 - core) * head
+    far_lane = (2 * far_col + core) * head
+    diag_lane = (2 * far_col + 1 - core) * head
+    for n_q, n_kv, lane, dev in (
+        (10, 13, near_lane, at_near), (11, 14, far_lane, at_far), (9, 12, diag_lane, at_diag)
+    ):
+        to = packed.at[:, lanes(lane, DH)]
+        rc(to, to, n_q, dev).wait_recv()
+        to = packed.at[:, lanes(lane + DH, 2 * DH)]
+        rc(to, to, n_kv, dev).wait_recv()
+
+    width = grad_ref.shape[1] // CHUNKS
+
+    def zcopy(kind, src, dst, k, dev):
+        return pltpu.make_async_remote_copy(
+            src_ref=src.at[k], dst_ref=dst.at[k], send_sem=zs.at[kind, k], recv_sem=zr.at[kind, k],
+            device_id=dev, device_id_type=MESH,
+        )
+
+    def product(k):
+        rows = pl.ds(pl.multiple_of(k * width, width), width)
+        return dot(packed[...], w_ref[rows, :], NT)
+
+    def put(k, value):
+        grad_ref[:, lanes(k * width, width)] = value
+
+    @pl.when(jnp.logical_not(is_mid))
+    def _():
+        @pl.loop(0, CHUNKS)
+        def _(k):
+            z_own[k] = product(k).astype(jnp.bfloat16)
+            zcopy(0, z_own, z_edge, k, at_side).start()
+
+        @pl.loop(0, CHUNKS)
+        def _(k):
+            zcopy(2, z_tot, z_tot, k, at_side).wait_recv()
+            put(k, z_tot[k])
+            zcopy(0, z_own, z_edge, k, at_side).wait_send()
+
+    @pl.when(is_mid)
+    def _():
+        def finish(k):
+            zcopy(1, z_own, z_mid, k, at_mid).wait_recv()
+            total = (z_own[k].astype(jnp.float32) + z_mid[k].astype(jnp.float32)).astype(jnp.bfloat16)
+            z_tot[k] = total
+            zcopy(2, z_tot, z_tot, k, at_side).start()
+            put(k, total)
+
+        @pl.loop(0, CHUNKS)
+        def _(k):
+            term = product(k)
+            zcopy(0, z_own, z_edge, k, at_side).wait_recv()
+            z_own[k] = (term + z_edge[k].astype(jnp.float32)).astype(jnp.bfloat16)
+            zcopy(1, z_own, z_mid, k, at_mid).start()
+
+            @pl.when(k > 0)
+            def _():
+                finish(k - 1)
+
+        finish(CHUNKS - 1)
+
+        @pl.loop(0, CHUNKS)
+        def _(k):
+            zcopy(1, z_own, z_mid, k, at_mid).wait_send()
+            zcopy(2, z_tot, z_tot, k, at_side).wait_send()
+
+    for copy in sent:
+        copy.wait_send()
+
+
+def fused(inputs, qkv_weight, out_cotangent):
+    tok, wide = inputs.shape
+    low, full = jnp.bfloat16, jnp.float32
+    head = 3 * DH
+    chunk = (CHUNKS, tok, wide // CHUNKS)
+    vmem = pl.BlockSpec(memory_space=pltpu.VMEM)
+    shapes = [
+        (inputs.shape, low), (qkv_weight.shape, low), (out_cotangent.shape, low),
+        ((2, tok, 2 * DH), full), ((2, tok, DH), full), ((2, tok, 2 * DH), full), ((2, tok, DH), full),
+        ((2, tok, head), full), ((tok, head), full),
+        ((2 * tok, DH), low), ((2 * tok, DH), low), ((4 * tok, 2 * DH), low),
+        ((2 * tok, 4 * tok), full), ((2 * tok, 4 * tok), full),
+        ((2 * tok, 4 * tok), low), ((2 * tok, 4 * tok), low),
+        ((tok, DH), low), ((tok, DH), low), ((tok, DH), low), ((2 * tok, DH), low),
+        ((2 * tok, 2 * DH), low), ((2 * tok, 2 * DH), low), ((2 * tok, 2 * DH), full),
+        ((2 * tok, 2 * DH), low), ((tok, 4 * head), low),
+        (chunk, low), (chunk, low), (chunk, low), (chunk, low),
+    ]
+    return pl.pallas_call(
+        block_kernel,
+        out_shape=(
+            jax.ShapeDtypeStruct(out_cotangent.shape, low),
+            jax.ShapeDtypeStruct(inputs.shape, low),
+        ),
+        in_specs=[pl.BlockSpec(memory_space=pl.ANY)] * 3,
+        out_specs=(vmem, vmem),
+        scratch_shapes=[pltpu.VMEM(shape, kind) for shape, kind in shapes]
+        + [pltpu.SemaphoreType.DMA((17,))] * 2
+        + [pltpu.SemaphoreType.DMA((3, CHUNKS))] * 2
+        + [pltpu.SemaphoreType.DMA((4,))],
+        compiler_params=pltpu.CompilerParams(
+            collective_id=0, has_side_effects=True, vmem_limit_bytes=62 * 1024 * 1024
+        ),
+    )(inputs, qkv_weight, out_cotangent)
+
+
+def block(inputs, qkv_weight, out_cotangent):
+    sizes = tuple(lax.axis_size(name) for name in ("ctx", "row", "col"))
+    heads = qkv_weight.shape[1] // (3 * DH)
+    if sizes == (4, 4, 2) and heads == 4 and inputs.shape[0] <= 256:
+        return fused(inputs, qkv_weight, out_cotangent)
+    return shards(inputs, qkv_weight, out_cotangent)
+
+
 def solution(mesh):
     return jax.shard_map(
-        shards,
+        block,
         mesh=mesh,
         in_specs=(P("ctx", "col"), P("col", "row"), P("ctx", ("row", "col"))),
         out_specs=(P("ctx", ("row", "col")), P("ctx", "col")),

time: 196 us -> 86.9 us (0.44)
  blocking collectives: 123 us -> 0 us
  Pallas kernels: 0 us -> 82.2 us
  waiting for transfers between devices: 30.1 us -> 0 us
  matrix products: 21 us -> 0 us
  between operations: 14.2 us -> 0.64 us
  other arithmetic: 2.43 us -> 0 us
    pallas_call x0 -> x1, Pallas kernels: none -> 82.2 us  [fused(): pl.pallas_call(block_kernel, out_shape=(jax.ShapeDtypeStruct(out_cotangen...]
    psum x1 -> x0, blocking collectives: 77.3 us -> none  [shards(): input_grad = lax.psum(local_sum, 'row').astype(jnp.bfloat16)]
    all_gather x6 -> x0, blocking collectives: 46 us -> none  [the longest x1 12 us: shards(): lax.all_gather(grad_packed, 'col', axis=0, tiled=True)]
    reduce_scatter x1 -> x0, waiting for transfers between devices: 28.9 us -> none  [shards(): lax.psum_scatter(lax.dot_general(panel_cols, inputs, (((0,), (1,)), ((),...]
    dot_general x8 -> x0, matrix products: 21 us -> none  [the longest x1 5.79 us: shards(): lax.dot_general(panel_cols, inputs, (((0,), (1,)), ((), ())), preferred_e...]
    unnamed x27 -> x2, local copies, waits for them, and re-layouts: 4.13 us -> 3.87 us
  transfers between devices with their start and end apart: 2 -> 0, of which waited for: 2 -> 0; matrix products, arithmetic and copies ran while one was open for 0% -> 0% of each run, Pallas kernels for 0% -> 0%
where the time goes in v1:
time: 86.9 us; the launch traced here: 86.7 us
  Pallas kernels  82.2 us (95%)
  local copies, waits for them, and re-layouts  3.87 us (4%)
    pallas_call x1, Pallas kernels, fused(): pl.pallas_call(block_kernel, out_shape=(jax.ShapeDtypeStruct(out_cotangen...  82.2 us
    unnamed x2, local copies, waits for them, and re-layouts  3.87 us

profile of v1, /device:TPU:0, one launch (start us, length us, event | category | flops | bytes accessed | tf_op | source)
XLA Modules:
  0.0 86.7 jit_solution(9381882538316497761)
XLA Ops:
  0.6 82.2 %shard_map.50 = (bf16[256,256]{1,0:T(8,128)(2,1)}, bf16[256,2048]{1,0:T(8,128)(2,1)}) custom-call(bf16[256,2048]{1,0:T(8,128)(2,1)} %x_hbm.1, bf16[2048,1536]{1,0:T(8,128)(2,1)} %w_hbm.1, bf16[256,256]{1,0:T(8,128)(2,1)} %cot_hbm.1), custom_call_target="tpu_custom_call" | custom-call | tf_op jit(solution)/shard_map/pallas_call | solution.py:368
  82.9 1.6 %copy.7 = bf16[256,256]{1,0:T(8,128)(2,1)} copy(bf16[256,256]{1,0:T(8,128)(2,1)} %get-tuple-element.4) | data formatting | bytes 262144
  84.4 2.3 %copy.8 = bf16[256,2048]{1,0:T(8,128)(2,1)} copy(bf16[256,2048]{1,0:T(8,128)(2,1)} %get-tuple-element.5) | data formatting | bytes 2097152

commit v2 on v1

--- a/solution.py
+++ b/solution.py
@@ -100,6 +100,7 @@
 
 MESH = pl.DeviceIdType.MESH
 CHUNKS = 16
+LAG = 2
 NN = (((1,), (0,)), ((), ()))
 NT = (((1,), (1,)), ((), ()))
 TN = (((0,), (0,)), ((), ()))
@@ -110,12 +111,12 @@
 
 
 def block_kernel(
-    x_hbm, w_hbm, cot_hbm, att_ref, grad_ref,
-    x_ref, w_ref, cot_ref, far_kv, far_q, got_kv, got_q, part_near, got_near, cot_all, query, kv, score, gscore,
+    x_ref, w_hbm, cot_ref, att_ref, grad_ref,
+    w_ref, far_kv, far_q, got_kv, got_q, part_near, got_near, cot_all, query, kv, score, gscore,
     prob_low, ds_low, att_mine, att_send, att_got, dq_send, dkv_send, dkv_got, dkv_own,
     dkv_out, packed, z_own, z_edge, z_mid, z_tot, ss, rs, zs, zr, ls,
 ):
-    tok = x_hbm.shape[0]
+    tok = x_ref.shape[0]
     head = 3 * DH
     scaling = 1.0 / math.sqrt(DH)
     ctx, row, col = lax.axis_index("ctx"), lax.axis_index("row"), lax.axis_index("col")
@@ -145,10 +146,8 @@
     far_w = lanes(far_col * 2 * head, 2 * head)
     own_w = lanes(col * 2 * head, 2 * head)
     loads = [
-        pltpu.make_async_copy(x_hbm, x_ref, ls.at[0]),
-        pltpu.make_async_copy(w_hbm.at[:, far_w], w_ref.at[:, far_w], ls.at[1]),
-        pltpu.make_async_copy(w_hbm.at[:, own_w], w_ref.at[:, own_w], ls.at[2]),
-        pltpu.make_async_copy(cot_hbm, cot_ref, ls.at[3]),
+        pltpu.make_async_copy(w_hbm.at[:, far_w], w_ref.at[:, far_w], ls.at[0]),
+        pltpu.make_async_copy(w_hbm.at[:, own_w], w_ref.at[:, own_w], ls.at[1]),
     ]
     for load in loads:
         load.start()
@@ -161,7 +160,6 @@
         pl.semaphore_signal(barrier, inc=1, device_id=at_mid, device_id_type=MESH)
 
     loads[0].wait()
-    loads[1].wait()
     far = dot(x_ref[...], w_ref[:, far_w], NN)
     for n in range(2):
         far_q[n] = far[:, n * head : n * head + DH]
@@ -186,9 +184,8 @@
     kv_copies.append(go(rc(far_kv.at[1 - core], got_kv.at[1], 1, at_diag)))
     q_copies = [go(rc(far_q.at[core], got_q.at[0], 15, at_far))]
     q_copies.append(go(rc(far_q.at[1 - core], got_q.at[1], 16, at_diag)))
-    loads[3].wait()
     cc = go(rc(cot_ref.at[:, lanes((1 - core) * DH, DH)], cot_all.at[pl.ds(tok, tok)], 3, at_near))
-    loads[2].wait()
+    loads[1].wait()
     own = dot(x_ref[...], w_ref[:, own_w], NN)
     part_near[0] = own[:, :head]
     part_near[1] = own[:, head:]
@@ -238,13 +235,22 @@
             )
             ds = (p * (gscore[here, :] - delta)).astype(jnp.bfloat16)
             ds_low[here, :] = ds
-            dq_send[here, :] = (dot(ds, kv[:, :DH], NN) * scaling).astype(jnp.bfloat16)
             if t == 1:
                 att_send[local, :] = att
             else:
                 att_mine[local, :] = att
+
+    dkv_copies = []
+    for t in range(2):
+        keys = pl.ds((2 + t) * tok, tok)
+        here = pl.ds(t * tok, tok)
+        dkv_send[here, :DH] = (dot(ds_low[:, keys], query[...], TN) * scaling).astype(jnp.bfloat16)
+        dkv_send[here, DH:] = dot(prob_low[:, keys], cot_all[...], TN).astype(jnp.bfloat16)
+        dkv_copies.append(go(rc(dkv_send.at[here], dkv_got.at[here], 6 + t, at_x)))
+    for t in (1, 0):
         here = pl.ds(t * tok, tok)
         slot = packed.at[:, lanes(mine_lane, DH)]
+        dq_send[here, :] = (dot(ds_low[here, :], kv[:, :DH], NN) * scaling).astype(jnp.bfloat16)
         if t == 1:
             go(rc(dq_send.at[here], slot, 9, at_diag))
             go(rc(dq_send.at[here], slot, 10, at_near))
@@ -252,14 +258,6 @@
         else:
             go(rc(dq_send.at[here], slot, 11, at_far))
             packed[:, lanes(mine_lane, DH)] = dq_send[here, :]
-
-    dkv_copies = []
-    for t in range(2):
-        keys = pl.ds((2 + t) * tok, tok)
-        here = pl.ds(t * tok, tok)
-        dkv_send[here, :DH] = (dot(ds_low[:, keys], query[...], TN) * scaling).astype(jnp.bfloat16)
-        dkv_send[here, DH:] = dot(prob_low[:, keys], cot_all[...], TN).astype(jnp.bfloat16)
-        dkv_copies.append(go(rc(dkv_send.at[here], dkv_got.at[here], 6 + t, at_x)))
     dkv_own[:, :DH] = dot(ds_low[:, near_keys], query[...], TN) * scaling
     dkv_own[:, DH:] = dot(prob_low[:, near_keys], cot_all[...], TN)
     att_copy.wait_recv()
@@ -332,11 +330,13 @@
             z_own[k] = (term + z_edge[k].astype(jnp.float32)).astype(jnp.bfloat16)
             zcopy(1, z_own, z_mid, k, at_mid).start()
 
-            @pl.when(k > 0)
+            @pl.when(k >= LAG)
             def _():
-                finish(k - 1)
-
-        finish(CHUNKS - 1)
+                finish(k - LAG)
+
+        @pl.loop(CHUNKS - LAG, CHUNKS)
+        def _(k):
+            finish(k)
 
         @pl.loop(0, CHUNKS)
         def _(k):
@@ -354,7 +354,7 @@
     chunk = (CHUNKS, tok, wide // CHUNKS)
     vmem = pl.BlockSpec(memory_space=pltpu.VMEM)
     shapes = [
-        (inputs.shape, low), (qkv_weight.shape, low), (out_cotangent.shape, low),
+        (qkv_weight.shape, low),
         ((2, tok, 2 * DH), full), ((2, tok, DH), full), ((2, tok, 2 * DH), full), ((2, tok, DH), full),
         ((2, tok, head), full), ((tok, head), full),
         ((2 * tok, DH), low), ((2 * tok, DH), low), ((4 * tok, 2 * DH), low),
@@ -371,14 +371,14 @@
             jax.ShapeDtypeStruct(out_cotangent.shape, low),
             jax.ShapeDtypeStruct(inputs.shape, low),
         ),
-        in_specs=[pl.BlockSpec(memory_space=pl.ANY)] * 3,
+        in_specs=[vmem, pl.BlockSpec(memory_space=pl.ANY), vmem],
         out_specs=(vmem, vmem),
         scratch_shapes=[pltpu.VMEM(shape, kind) for shape, kind in shapes]
         + [pltpu.SemaphoreType.DMA((17,))] * 2
         + [pltpu.SemaphoreType.DMA((3, CHUNKS))] * 2
-        + [pltpu.SemaphoreType.DMA((4,))],
+        + [pltpu.SemaphoreType.DMA((2,))],
         compiler_params=pltpu.CompilerParams(
-            collective_id=0, has_side_effects=True, vmem_limit_bytes=62 * 1024 * 1024
+            collective_id=0, has_side_effects=True, vmem_limit_bytes=48 * 1024 * 1024
         ),
     )(inputs, qkv_weight, out_cotangent)
 

time: 86.9 us -> 77.3 us (0.89)
  Pallas kernels: 82.2 us -> 72.7 us
    pallas_call x1, Pallas kernels: 82.2 us -> 72.7 us  [fused(): pl.pallas_call(block_kernel, out_shape=(jax.ShapeDtypeStruct(out_cotangen...]
    unnamed x2 -> x6, local copies, waits for them, and re-layouts: 3.87 us -> 3.75 us
where the time goes in v2:
time: 77.3 us; the launch traced here: 77.1 us
  Pallas kernels  72.7 us (94%)
  local copies, waits for them, and re-layouts  3.75 us (5%)
    pallas_call x1, Pallas kernels, fused(): pl.pallas_call(block_kernel, out_shape=(jax.ShapeDtypeStruct(out_cotangen...  72.7 us
    unnamed x6, local copies, waits for them, and re-layouts  3.75 us

profile of v2, /device:TPU:0, one launch (start us, length us, event | category | flops | bytes accessed | tf_op | source)
XLA Modules:
  0.0 77.1 jit_solution(6104322897615250996)
XLA Ops:
  0.6 0.0 copy-start
  0.6 1.2 %copy-done = bf16[256,2048]{1,0:T(8,128)(2,1)S(1)} copy-done((bf16[256,2048]{1,0:T(8,128)(2,1)S(1)}, bf16[256,2048]{1,0:T(8,128)(2,1)}, u32[]{:S(2)}) %copy-start) | copy-done | bytes 1048600
  1.9 0.0 copy-start.1
  1.9 0.9 %copy-done.1 = bf16[256,256]{1,0:T(8,128)(2,1)S(1)} copy-done((bf16[256,256]{1,0:T(8,128)(2,1)S(1)}, bf16[256,256]{1,0:T(8,128)(2,1)}, u32[]{:S(2)}) %copy-start.1) | copy-done | bytes 131096
  2.8 72.7 %shard_map.50 = (bf16[256,256]{1,0:T(8,128)(2,1)S(1)}, bf16[256,2048]{1,0:T(8,128)(2,1)S(1)}) custom-call(bf16[256,2048]{1,0:T(8,128)(2,1)S(1)} %copy-done, bf16[2048,1536]{1,0:T(8,128)(2,1)} %w_hbm.1, bf16[256,256]{1,0:T(8,128)(2,1)S(1)} %copy-done.1), custom_call_target="tpu_custom_call" | custom-call | tf_op jit(solution)/shard_map/pallas_call | solution.py:368
  75.5 0.7 copy.7
  76.1 1.0 %copy.8 = bf16[256,2048]{1,0:T(8,128)(2,1)} copy(bf16[256,2048]{1,0:T(8,128)(2,1)S(1)} %get-tuple-element.5) | data formatting | bytes 2097152
Async XLA Ops:
  0.6 1.2 %copy-start = (bf16[256,2048]{1,0:T(8,128)(2,1)S(1)}, bf16[256,2048]{1,0:T(8,128)(2,1)}, u32[]{:S(2)}) copy-start(bf16[256,2048]{1,0:T(8,128)(2,1)} %x_ref.1) | copy-start | bytes 3145732
  1.9 0.9 %copy-start.1 = (bf16[256,256]{1,0:T(8,128)(2,1)S(1)}, bf16[256,256]{1,0:T(8,128)(2,1)}, u32[]{:S(2)}) copy-start(bf16[256,256]{1,0:T(8,128)(2,1)} %cot_ref.1) | copy-start | bytes 393220

commit v3 on v2

--- a/solution.py
+++ b/solution.py
@@ -143,11 +143,12 @@
     def lanes(start, size):
         return pl.ds(pl.multiple_of(start, 128), size)
 
-    far_w = lanes(far_col * 2 * head, 2 * head)
+    far_heads = ((2 * far_col + core) * head, (2 * far_col + 1 - core) * head)
+    far_parts = [lanes(n + DH, 2 * DH) for n in far_heads] + [lanes(n, DH) for n in far_heads]
     own_w = lanes(col * 2 * head, 2 * head)
     loads = [
-        pltpu.make_async_copy(w_hbm.at[:, far_w], w_ref.at[:, far_w], ls.at[0]),
-        pltpu.make_async_copy(w_hbm.at[:, own_w], w_ref.at[:, own_w], ls.at[1]),
+        pltpu.make_async_copy(w_hbm.at[:, part], w_ref.at[:, part], ls.at[n])
+        for n, part in enumerate(far_parts + [own_w])
     ]
     for load in loads:
         load.start()
@@ -160,10 +161,7 @@
         pl.semaphore_signal(barrier, inc=1, device_id=at_mid, device_id_type=MESH)
 
     loads[0].wait()
-    far = dot(x_ref[...], w_ref[:, far_w], NN)
-    for n in range(2):
-        far_q[n] = far[:, n * head : n * head + DH]
-        far_kv[n] = far[:, n * head + DH : (n + 1) * head]
+    far_kv[0] = dot(x_ref[...], w_ref[:, far_parts[0]], NN)
 
     @pl.when(is_mid)
     def _():
@@ -180,12 +178,17 @@
         sent.append(copy)
         return copy
 
-    kv_copies = [go(rc(far_kv.at[core], got_kv.at[0], 0, at_far))]
-    kv_copies.append(go(rc(far_kv.at[1 - core], got_kv.at[1], 1, at_diag)))
-    q_copies = [go(rc(far_q.at[core], got_q.at[0], 15, at_far))]
-    q_copies.append(go(rc(far_q.at[1 - core], got_q.at[1], 16, at_diag)))
+    kv_copies = [go(rc(far_kv.at[0], got_kv.at[0], 0, at_far))]
+    loads[1].wait()
+    far_kv[1] = dot(x_ref[...], w_ref[:, far_parts[1]], NN)
+    kv_copies.append(go(rc(far_kv.at[1], got_kv.at[1], 1, at_diag)))
+    q_copies = []
+    for n, dev in enumerate((at_far, at_diag)):
+        loads[2 + n].wait()
+        far_q[n] = dot(x_ref[...], w_ref[:, far_parts[2 + n]], NN)
+        q_copies.append(go(rc(far_q.at[n], got_q.at[n], 15 + n, dev)))
     cc = go(rc(cot_ref.at[:, lanes((1 - core) * DH, DH)], cot_all.at[pl.ds(tok, tok)], 3, at_near))
-    loads[1].wait()
+    loads[4].wait()
     own = dot(x_ref[...], w_ref[:, own_w], NN)
     part_near[0] = own[:, :head]
     part_near[1] = own[:, head:]
@@ -376,7 +379,7 @@
         scratch_shapes=[pltpu.VMEM(shape, kind) for shape, kind in shapes]
         + [pltpu.SemaphoreType.DMA((17,))] * 2
         + [pltpu.SemaphoreType.DMA((3, CHUNKS))] * 2
-        + [pltpu.SemaphoreType.DMA((2,))],
+        + [pltpu.SemaphoreType.DMA((5,))],
         compiler_params=pltpu.CompilerParams(
             collective_id=0, has_side_effects=True, vmem_limit_bytes=48 * 1024 * 1024
         ),

time: 77.3 us -> 76.2 us (0.986)
  Pallas kernels: 72.7 us -> 71.6 us
    pallas_call x1, Pallas kernels: 72.7 us -> 71.6 us  [fused(): pl.pallas_call(block_kernel, out_shape=(jax.ShapeDtypeStruct(out_cotangen...]
where the time goes in v3:
time: 76.2 us; the launch traced here: 76 us
  Pallas kernels  71.6 us (94%)
  local copies, waits for them, and re-layouts  3.75 us (5%)
    pallas_call x1, Pallas kernels, fused(): pl.pallas_call(block_kernel, out_shape=(jax.ShapeDtypeStruct(out_cotangen...  71.6 us
    unnamed x6, local copies, waits for them, and re-layouts  3.75 us

profile of v3, /device:TPU:0, one launch (start us, length us, event | category | flops | bytes accessed | tf_op | source)
XLA Modules:
  0.0 76.0 jit_solution(4858851473448456076)
XLA Ops:
  0.6 0.0 copy-start
  0.6 1.2 %copy-done = bf16[256,2048]{1,0:T(8,128)(2,1)S(1)} copy-done((bf16[256,2048]{1,0:T(8,128)(2,1)S(1)}, bf16[256,2048]{1,0:T(8,128)(2,1)}, u32[]{:S(2)}) %copy-start) | copy-done | bytes 1048600
  1.9 0.0 copy-start.1
  1.9 0.9 %copy-done.1 = bf16[256,256]{1,0:T(8,128)(2,1)S(1)} copy-done((bf16[256,256]{1,0:T(8,128)(2,1)S(1)}, bf16[256,256]{1,0:T(8,128)(2,1)}, u32[]{:S(2)}) %copy-start.1) | copy-done | bytes 131096
  2.8 71.6 %shard_map.50 = (bf16[256,256]{1,0:T(8,128)(2,1)S(1)}, bf16[256,2048]{1,0:T(8,128)(2,1)S(1)}) custom-call(bf16[256,2048]{1,0:T(8,128)(2,1)S(1)} %copy-done, bf16[2048,1536]{1,0:T(8,128)(2,1)} %w_hbm.1, bf16[256,256]{1,0:T(8,128)(2,1)S(1)} %copy-done.1), custom_call_target="tpu_custom_call" | custom-call | tf_op jit(solution)/shard_map/pallas_call | solution.py:371
  74.4 0.7 copy.7
  75.0 1.0 %copy.8 = bf16[256,2048]{1,0:T(8,128)(2,1)} copy(bf16[256,2048]{1,0:T(8,128)(2,1)S(1)} %get-tuple-element.5) | data formatting | bytes 2097152
Async XLA Ops:
  0.6 1.2 %copy-start = (bf16[256,2048]{1,0:T(8,128)(2,1)S(1)}, bf16[256,2048]{1,0:T(8,128)(2,1)}, u32[]{:S(2)}) copy-start(bf16[256,2048]{1,0:T(8,128)(2,1)} %x_ref.1) | copy-start | bytes 3145732
  1.9 0.9 %copy-start.1 = (bf16[256,256]{1,0:T(8,128)(2,1)S(1)}, bf16[256,256]{1,0:T(8,128)(2,1)}, u32[]{:S(2)}) copy-start(bf16[256,256]{1,0:T(8,128)(2,1)} %cot_ref.1) | copy-start | bytes 393220
